TPU v7x, 512 devices: a whole 4x8x8 slice. The times are simulated.
512 devices in a mesh: row: 16 (over x, y_hi), col: 32 (over y_lo, z, core).
Axes of the slice: x: 4, y: 8 (y_hi: 4, y_lo: 2; y = y_hi * 2 + y_lo), z: 8, core: 2. Of those that a mesh axis runs over, the one named last changes fastest.
Arguments:
- phase: float32 [6, 262144], P(None, ('row', 'col')), may hold values from -6 to 6
- masses: float32 [1, 262144], P(None, ('row', 'col')), may hold values from 0.1 to 10
- active_index: int32 [8192], P('col'), may hold values from 0 to 262143, as said below
Outputs:
- accel: float32 [3, 8192], P(None, 'col')
- jerk: float32 [3, 8192], P(None, 'col')
Inputs may be any that keep to these rules, and one draw needn't show every extreme that they name: `active_index`: distinct star indices; 0 and 262143 are always among them.
All inputs are finite; a program needn't handle non-finite values.
Results may differ from a plain program's by a relative error of at most 0.0003.
Values sent between devices are 32-bit elements; how exact they have to be, the bound alone decides.
No kernel may reach another device: no remote copies, remote signals or barrier semaphores. Data moves between devices by JAX's collectives and lax.ppermute only.
A program may use at most 64 MiB of HBM per device.

v0:
```python
import jax
import jax.numpy as jnp
from jax import lax
from jax.sharding import PartitionSpec as P

SOFTEN_SQ = 0.0001


def pair_terms(active_state, field_block):
    offset = field_block[0:3, None, :] - active_state[0:3, :, None]
    relative = field_block[3:6, None, :] - active_state[3:6, :, None]
    distance_sq = jnp.sum(offset * offset, axis=0) + SOFTEN_SQ
    inverse = lax.rsqrt(distance_sq)
    weight = field_block[6][None, :] * inverse * inverse * inverse
    radial_rate = 3.0 * jnp.sum(offset * relative, axis=0) / distance_sq
    accel_sum = jnp.sum(weight[None] * offset, axis=2)
    jerk_sum = jnp.sum(weight[None] * (relative - radial_rate[None] * offset), axis=2)
    return jnp.concatenate([accel_sum, jerk_sum], axis=0)


def block_terms(active_state, field_block, shard_width):
    width = min(shard_width, field_block.shape[1])
    count = field_block.shape[1] // width
    stacked = jnp.transpose(field_block.reshape(7, count, width), (1, 0, 2))

    def add_one(running, single):
        return (running + pair_terms(active_state, single), None)

    start_value = jnp.zeros((6, active_state.shape[1]), jnp.float32)
    running, _ = lax.scan(add_one, start_value, stacked)
    return running


def local(phase, masses, active_index):
    shard_width = phase.shape[1]
    rows_count = lax.axis_size("row")
    cols_count = lax.axis_size("col")
    inverse_count = 1.0 / (shard_width * rows_count * cols_count)
    field_block = jnp.concatenate([phase, masses], axis=0)
    all_index = lax.all_gather(active_index, "col", axis=0, tiled=True)
    shard_start = (lax.axis_index("row") * cols_count + lax.axis_index("col")) * shard_width
    local_index = all_index - shard_start
    inside_mask = ((local_index >= 0) & (local_index < shard_width)).astype(jnp.float32)
    picked = (
        jnp.take(phase, jnp.clip(local_index, 0, shard_width - 1), axis=1) * inside_mask[None, :]
    )
    own_count = active_index.shape[0]
    active_table = lax.psum(picked, ("row", "col"))
    active_state = lax.dynamic_slice_in_dim(
        active_table, lax.axis_index("col") * own_count, own_count, 1
    )
    partial_sum = block_terms(
        active_state, lax.all_gather(field_block, "col", axis=1, tiled=True), shard_width
    )
    total = lax.psum(partial_sum, "row")
    total = total * inverse_count
    return (total[0:3], total[3:6])


def solution(mesh):
    placed = (P(None, ("row", "col")), P(None, ("row", "col")), P("col"))
    return jax.shard_map(
        local,
        mesh=mesh,
        in_specs=placed,
        out_specs=(P(None, "col"), P(None, "col")),
        check_vma=False,
    )
```

profile of v0, /device:TPU:8, one launch (start us, length us, event | category | flops | bytes accessed | tf_op | source)
XLA Modules:
  0.0 464.2 jit_solution(118549759133231043)
XLA Ops:
  7.2 39.6 %all-gather = s32[32,1,256]{2,1,0:T(1,128)S(1)} all-gather(s32[1,1,256]{2,1,0:T(1,128)} %bitcast.22), channel_id=1, replica_groups=mesh['row'=16,'col'=32] {'col'}, dimensions={0}, use_global_device_ids=true | all-gather | bytes 33792 | tf_op jit(solution)/shard_map/all_gather | solution.py:40
  46.9 0.9 copy.9
  47.8 27.7 %gather_fusion = f32[8192,6]{1,0:T(8,128)} fusion(f32[6,512]{0,1:T(8,128)S(1)} %copy.9, s32[8192]{0:T(1024)S(1)} %fusion.5), kind=kCustom, calls=%fused_computation | custom fusion | bytes 425984 | tf_op jit(solution)/shard_map/jit(_take)/gather | solution.py:45
  75.5 9.7 %multiply_bitcast_fusion = f32[6,8192]{0,1:T(8,128)} fusion(f32[8192,6]{1,0:T(8,128)} %gather_fusion, f32[8192]{0:T(1024)S(1)} %bitcast.21, pred[8192]{0:T(1024)(128)(4,1)S(1)} %compare_and_fusion), kind=kLoop, calls=%fused_computation.17 | loop fusion | flops 98304 | bytes 434176 | tf_op jit(solution)/shard_map/mul | solution.py:45
  85.9 32.2 %all_gather.6 = f32[7,16384]{1,0:T(8,128)S(1)} all-gather(f32[7,512]{1,0:T(8,128)S(1)} %pad_maximum_fusion), channel_id=1, replica_groups=mesh['row'=16,'col'=32] {'col'}, dimensions={1}, use_global_device_ids=true | all-gather | bytes 473088 | tf_op jit(solution)/shard_map/all_gather | solution.py:53
  118.2 248.5 %all-reduce.2.cloned.1.call-done = f32[6,8192]{0,1:T(8,128)} async-done(((f32[6,8192]{0,1:T(8,128)}), f32[6,8192]{0,1:T(8,128)}) %all-reduce.2.cloned.1.call-update) | async-done | bytes 196624 | tf_op jit(solution)/shard_map/psum | solution.py:48
  366.7 0.9 constant_dynamic-slice_fusion.1
  367.7 43.6 %while.11 = (s32[]{:T(128)}, f32[6,256]{1,0:T(8,128)S(1)}, f32[32,7,512]{2,1,0:T(8,128)S(1)}, f32[6,256]{1,0:T(8,128)S(1)}, s32[]{:T(128)}, /*index=5*/s32[]{:T(128)}, s32[]{}, s32[]{}) while((s32[]{:T(128)}, f32[6,256]{1,0:T(8,128)S(1)}, f32[32,7,512]{2,1,0:T(8,128)S(1)}, f32[6,256]{1,0:T(8,128)S(1)}, s32[]{:T(128)}, ...), condition=%wide.region_6.7_spmd.clone, body=%wide.region_1.6_spmd.clone.sunk | while | flops 6032389 | bytes 4298887 | solution.py:30
  369.6 0.7 fusion.13
  372.3 0.7 fusion.13
  373.7 0.7 fusion.13
  375.1 0.7 fusion.13
  376.4 0.7 fusion.13
  377.8 0.7 fusion.13
  379.2 0.7 fusion.13
  380.5 0.7 fusion.13
  381.9 0.7 fusion.13
  384.6 0.7 fusion.13
  387.4 0.7 fusion.13
  390.1 0.7 fusion.13
  392.8 0.7 fusion.13
  395.5 0.7 fusion.13
  398.3 0.7 fusion.13
  399.6 0.7 fusion.13
  401.0 0.7 fusion.13
  402.4 0.7 fusion.13
  403.7 0.7 fusion.13
  405.1 0.7 fusion.13
  406.5 0.7 fusion.13
  407.8 0.7 fusion.13
  410.5 0.7 fusion.13
  411.3 45.4 %psum.15 = f32[6,256]{1,0:T(8,128)S(1)} all-reduce(f32[6,256]{1,0:T(8,128)S(1)} %get-tuple-element.24), channel_id=1, replica_groups=mesh['row'=16,'col'=32] {'row'}, use_global_device_ids=true, to_apply=%region_7.8 | all-reduce | flops 1536 | bytes 12288 | tf_op jit(solution)/shard_map/psum | solution.py:55
  (216 shorter events, 26.1 us)
Async XLA Ops:
  7.2 359.5 %all-reduce.2.cloned.1.call-start = ((), (), s32[]{:S(2)}) async-start(), calls=%async_computation | async-start | bytes 8388608 | tf_op jit(solution)/shard_map/psum | solution.py:48
  85.2 0.7 copy-start
  85.2 0.7 copy-start.1
Sparse Core Ops, SparseCore 0:
  85.4 281.2 all-reduce.1
where the time goes:
time: 465 us; the launch traced here: 464 us
  waiting for transfers between devices  249 us (54%)
  blocking collectives  117 us (25%)
  other arithmetic  50.6 us (11%)
  local copies, waits for them, and re-layouts  31.9 us (7%)
  between operations  14.1 us (3%)
    psum x1, waiting for transfers between devices, local(): active_table = lax.psum(picked, ('row', 'col'))  249 us
    psum x1, blocking collectives, local(): total = lax.psum(partial_sum, 'row')  45.4 us
    all_gather x1, blocking collectives, local(): all_index = lax.all_gather(active_index, 'col', axis=0, tiled=True)  39.6 us
    all_gather x1, blocking collectives, local(): lax.all_gather(field_block, 'col', axis=1, tiled=True)  32.2 us
    gather x1, local copies, waits for them, and re-layouts, local(): jnp.take(phase, jnp.clip(local_index, 0, shard_width - 1), axis=1)  27.7 us
    reduce_sum x32, other arithmetic, pair_terms(): accel_sum = jnp.sum(weight[None] * offset, axis=2)  24 us
    reduce_sum x32, other arithmetic, pair_terms(): distance_sq = jnp.sum(offset * offset, axis=0) + SOFTEN_SQ  11.7 us
    mul x1, other arithmetic, local(): jnp.take(phase, jnp.clip(local_index, 0, shard_width - 1), axis=1)  9.69 us
  transfers between devices with their start and end apart: 1, of which 1 were waited for; matrix products, arithmetic and copies ran while one was open for 0% of the time, Pallas kernels for 0%

commit v1 on v0

v1 whole, which is shorter than its diff:
```python
import functools

import jax
import jax.numpy as jnp
from jax import lax
from jax.experimental import pallas as pl
from jax.experimental.pallas import tpu as pltpu
from jax.sharding import Mesh, PartitionSpec as P

SOFTEN_SQ = 0.0001
NAMES = ("x", "yh", "yl", "z", "c")
ROW = ("x", "yh")
COL = ("yl", "z", "c")
LANES = 128
F32 = jnp.float32
BF16 = jnp.bfloat16


def pieces(value):
    high = value.astype(BF16)
    rest = value - high.astype(F32)
    middle = rest.astype(BF16)
    low = (rest - middle.astype(F32)).astype(BF16)
    return high, middle, low


def pick_kernel(slab_ref, place_ref, out_ref):
    blocks, _, width = slab_ref.shape
    count = place_ref.shape[1]
    block = place_ref[0:1, :]
    place = place_ref[1:2, :]
    one_hot = lax.broadcasted_iota(jnp.int32, (blocks, count), 0) == block
    one_hot = jnp.where(one_hot, 1.0, 0.0).astype(BF16)
    one_hot = jnp.concatenate([one_hot, one_hot, one_hot], axis=0)
    here = lax.broadcasted_iota(jnp.int32, (width, count), 0) == place
    rows = []
    for c in range(6):
        values = jnp.concatenate(pieces(slab_ref[:, c, :]), axis=0)
        taken = lax.dot_general(
            values, one_hot, (((0,), (0,)), ((), ())), preferred_element_type=F32
        )
        rows.append(jnp.sum(jnp.where(here, taken, 0.0), axis=0, keepdims=True))
    rows.append(jnp.zeros((2, count), F32))
    out_ref[...] = jnp.concatenate(rows, axis=0)


def field_kernel(slab_ref, sums_ref, dots_ref, centre_ref):
    blocks, _, width = slab_ref.shape
    total = jnp.zeros((8, width), F32)
    for b in range(blocks):
        total = total + slab_ref[b]
    row = lax.broadcasted_iota(jnp.int32, (8, 1), 0)
    mean = jnp.sum(total, axis=1, keepdims=True) * (1.0 / (blocks * width))
    centre = jnp.where(row < 6, mean, 0.0)
    centre_ref[...] = jnp.broadcast_to(centre, (8, LANES))
    rows = lax.broadcasted_iota(jnp.int32, (8, width), 0)
    for b in range(blocks):
        where = slice(b * width, (b + 1) * width)
        star = slab_ref[b] - centre
        mass = star[6:7, :]
        high, middle, low = pieces(jnp.where(rows == 6, mass, star * mass))
        sums_ref[:, where] = jnp.concatenate([high, middle, low, jnp.zeros_like(low)], axis=0)
        along = jnp.sum(star[0:3, :] * star[3:6, :], axis=0, keepdims=True)
        terms = jnp.where(rows == 6, along, star)
        terms = jnp.where(rows == 7, 1.0, terms)
        high, middle, low = pieces(terms)
        dots_ref[:, where] = jnp.concatenate([high, high, middle, middle, high, low], axis=0)


def pair_kernel(slab_ref, sums_ref, dots_ref, centre_ref, picks_ref, out_ref,
                spread, left, dot, terms, total, *, width, rows, lanes):
    count = picks_ref.shape[2]
    blocks, _, block_width = slab_ref.shape
    state = picks_ref[0]
    for p in range(1, picks_ref.shape[0]):
        state = state + picks_ref[p]
    columns = jnp.transpose(state)
    for c in range(3):
        spread[c] = jnp.broadcast_to(columns[:, c:c + 1], (count, LANES))
    local = state - centre_ref[:, 0:1]
    position, velocity = local[0:3, :], local[3:6, :]
    along = jnp.sum(position * velocity, axis=0, keepdims=True)
    ones = jnp.ones((1, count), F32)
    against = jnp.concatenate([-velocity, -position, ones, along], axis=0)
    high, middle, low = pieces(against)
    stack = [high, middle, high, middle, low, high]
    stack = jnp.concatenate([part.astype(F32) for part in stack], axis=0)
    left[...] = jnp.transpose(stack).astype(BF16)
    total[...] = jnp.zeros_like(total)

    def step(j, _):
        chunk = pl.ds(pl.multiple_of(j * width, width), width)
        dot[...] = jnp.dot(left[...], dots_ref[:, chunk], preferred_element_type=F32)
        for i in range(count // rows):
            here = slice(i * rows, (i + 1) * rows)
            active = [
                jnp.concatenate([spread[c, here, :]] * (lanes // LANES), axis=1)
                for c in range(3)
            ]
            for l in range(width // lanes):
                there = slice(l * lanes, (l + 1) * lanes)
                block = j * (width // block_width) + l * lanes // block_width
                start = l * lanes % block_width
                offset = [
                    slab_ref[block, c:c + 1, start:start + lanes] - active[c] for c in range(3)
                ]
                distance_sq = offset[0] * offset[0] + (
                    offset[1] * offset[1] + (offset[2] * offset[2] + SOFTEN_SQ)
                )
                inverse = lax.rsqrt(distance_sq)
                inverse_sq = inverse * inverse
                weight = inverse * inverse_sq
                rate = weight * (dot[here, there] * inverse_sq)
                for n, value in enumerate((weight, rate)):
                    high = value.astype(BF16)
                    low = (value - high.astype(F32)).astype(BF16)
                    at = 2 * n * count + i * rows
                    terms[at:at + rows, there] = high
                    terms[at + count:at + count + rows, there] = low
        total[...] += lax.dot_general(
            terms[...], sums_ref[:, chunk], (((1,), (1,)), ((), ())), preferred_element_type=F32
        )
        return 0

    lax.fori_loop(0, blocks * block_width // width, step, 0)
    sums = total[0:2 * count, :].reshape(2, count, 32)
    rates = total[2 * count:4 * count, :].reshape(2, count, 32)
    sums = jnp.transpose(sums[0] + sums[1])
    rates = jnp.transpose(rates[0] + rates[1])
    sums = sums[0:8, :] + sums[8:16, :] + sums[16:24, :]
    rates = rates[0:8, :] + rates[8:16, :] + rates[16:24, :]
    accel = sums[0:3, :] - position * sums[6:7, :]
    jerk = sums[3:6, :] - velocity * sums[6:7, :]
    jerk = jerk - 3.0 * (rates[0:3, :] - position * rates[6:7, :])
    out_ref[...] = jnp.concatenate([accel, jerk, jnp.zeros((2, count), F32)], axis=0)


def call(kernel, outs, scratch=(), name=None):
    return pl.pallas_call(
        kernel,
        out_shape=outs,
        scratch_shapes=list(scratch),
        compiler_params=pltpu.CompilerParams(vmem_limit_bytes=40 * 2**20),
        name=name,
    )


def spread_over(value, axes):
    size = lax.axis_size(axes)
    return lax.all_to_all(jnp.broadcast_to(value[None], (size,) + value.shape), axes, 0, 0)


def local(phase, masses, active_index):
    width = phase.shape[1]
    count = active_index.shape[0]
    rows_count, cols_count = lax.axis_size(ROW), lax.axis_size(COL)
    stars = width * rows_count * cols_count
    core = lax.axis_index("c")
    half = spread_over(jnp.concatenate([phase, masses, jnp.zeros_like(masses)], axis=0), ("yl", "z"))
    other = lax.ppermute(half, "c", [(0, 1), (1, 0)])
    slab = jnp.concatenate([half, other], axis=0)

    slab_width = width * cols_count
    block = active_index // width
    column = block % cols_count
    place = (column % 2 != core) * (cols_count // 2) + column // 2
    place = jnp.where(active_index // slab_width == lax.axis_index(ROW), place, -1)
    where = jnp.stack([place, active_index % width])

    picked = call(pick_kernel, jax.ShapeDtypeStruct((8, count), F32), name="pick")(slab, where)
    picks = spread_over(picked, ROW)
    sums, dots, centre = call(
        field_kernel,
        (
            jax.ShapeDtypeStruct((32, slab_width), BF16),
            jax.ShapeDtypeStruct((48, slab_width), BF16),
            jax.ShapeDtypeStruct((8, LANES), F32),
        ),
        name="field",
    )(slab)
    chunk = 1024
    partial = call(
        functools.partial(pair_kernel, width=chunk, rows=16, lanes=256),
        jax.ShapeDtypeStruct((8, count), F32),
        (
            pltpu.VMEM((3, count, LANES), F32),
            pltpu.VMEM((count, 48), BF16),
            pltpu.VMEM((count, chunk), F32),
            pltpu.VMEM((4 * count, chunk), BF16),
            pltpu.VMEM((4 * count, 32), F32),
        ),
        name="pairs",
    )(slab, sums, dots, centre, picks)
    total = jnp.sum(spread_over(partial[0:6], ROW), axis=0) * (1.0 / stars)
    return total[0:3], total[3:6]


def solution(mesh):
    fine = Mesh(mesh.devices.reshape(4, 4, 2, 8, 2), NAMES)
    stars = P(None, ROW + COL)
    return jax.shard_map(
        local,
        mesh=fine,
        in_specs=(stars, stars, P(COL)),
        out_specs=(P(None, COL), P(None, COL)),
        check_vma=False,
    )
```

time: 465 us -> 85.3 us (0.18)
  waiting for transfers between devices: 249 us -> 20.5 us
  blocking collectives: 117 us -> 13.4 us
  other arithmetic: 50.6 us -> 1.55 us
  local copies, waits for them, and re-layouts: 31.9 us -> 2.11 us
  Pallas kernels: 0 us -> 24 us
  starting transfers between devices: 0.04 us -> 22.5 us
  between operations: 14.1 us -> 0.7 us
    psum x1 -> x0, waiting for transfers between devices: 249 us -> none  [local(): active_table = lax.psum(picked, ('row', 'col'))]
    all_gather x2 -> x0, blocking collectives: 71.8 us -> none  [the longest x1 39.6 us: local(): all_index = lax.all_gather(active_index, 'col', axis=0, tiled=True)]
    psum x1 -> x0, blocking collectives: 45.4 us -> none  [local(): total = lax.psum(partial_sum, 'row')]
    reduce_sum x64 -> x1, other arithmetic: 35.7 us -> 0.02 us  [local(): total = jnp.sum(spread_over(partial[0:6], ROW), axis=0) * (1.0 / stars)]
    gather x1 -> x0, local copies, waits for them, and re-layouts: 27.7 us -> none  [local(): jnp.take(phase, jnp.clip(local_index, 0, shard_width - 1), axis=1)]
    pallas_call x0 -> x3, Pallas kernels: none -> 24 us  [the longest x1 20.4 us: local(): call(functools.partial(pair_kernel, width=chunk, rows=16, lanes=256), jax...]
    all_to_all x0 -> x2, starting transfers between devices: none -> 20.6 us  [spread_over(): lax.all_to_all(jnp.broadcast_to(value[None], (size,) + value.shape), axes...]
    all_to_all x0 -> x2, waiting for transfers between devices: none -> 19.8 us  [spread_over(): lax.all_to_all(jnp.broadcast_to(value[None], (size,) + value.shape), axes...]
  transfers between devices with their start and end apart: 1 -> 3, of which waited for: 1 -> 3; matrix products, arithmetic and copies ran while one was open for 0% -> 1% of each run, Pallas kernels for 0% -> 1%
where the time goes in v1:
time: 85.3 us; the launch traced here: 84.8 us
  Pallas kernels  24 us (28%)
  starting transfers between devices  22.5 us (26%)
  waiting for transfers between devices  20.5 us (24%)
  blocking collectives  13.4 us (16%)
  local copies, waits for them, and re-layouts  2.11 us (2%)
  other arithmetic  1.55 us (2%)
    all_to_all x2, starting transfers between devices, spread_over(): lax.all_to_all(jnp.broadcast_to(value[None], (size,) + value.shape), axes...  20.6 us
    pallas_call x1, Pallas kernels, local(): call(functools.partial(pair_kernel, width=chunk, rows=16, lanes=256), jax...  20.4 us
    all_to_all x2, waiting for transfers between devices, spread_over(): lax.all_to_all(jnp.broadcast_to(value[None], (size,) + value.shape), axes...  19.8 us
    all_to_all x1, blocking collectives, spread_over(): lax.all_to_all(jnp.broadcast_to(value[None], (size,) + value.shape), axes...  13.4 us
    pallas_call x1, Pallas kernels, local(): call(pick_kernel, jax.ShapeDtypeStruct((8, count), F32), name='pick')  2.78 us
    ppermute x1, starting transfers between devices, local(): other = lax.ppermute(half, 'c', [(0, 1), (1, 0)])  1.91 us
  transfers between devices with their start and end apart: 3, of which 3 were waited for; matrix products, arithmetic and copies ran while one was open for 1% of the time, Pallas kernels for 1%

profile of v1, /device:TPU:8, one launch (start us, length us, event | category | flops | bytes accessed | tf_op | source)
XLA Modules:
  0.0 84.8 jit_solution(813430527696756789)
XLA Ops:
  0.6 0.1 pad.4.clone
  0.7 0.8 maximum_maximum_fusion
  1.5 0.7 broadcast_in_dim.11
  2.2 11.8 %all-to-all-start = ((f32[16,8,512]{2,1,0:T(8,128)}), f32[16,8,512]{2,1,0:T(8,128)S(1)}, u32[]{:S(2)}, u32[]{:S(2)}) async-start(f32[16,8,512]{2,1,0:T(8,128)} %broadcast_in_dim.11), calls=%async_computation | async-start | bytes 524288 | tf_op jit(solution)/shard_map/all_to_all | solution.py:150
  14.0 9.3 %all-to-all-done = f32[16,8,512]{2,1,0:T(8,128)S(1)} async-done(((f32[16,8,512]{2,1,0:T(8,128)}), f32[16,8,512]{2,1,0:T(8,128)S(1)}, u32[]{:S(2)}, u32[]{:S(2)}) %all-to-all-start) | async-done | bytes 262176 | tf_op jit(solution)/shard_map/all_to_all | solution.py:150
  23.4 1.9 %collective-permute-start = (f32[16,8,512]{2,1,0:T(8,128)S(1)}, f32[16,8,512]{2,1,0:T(8,128)S(1)}, u32[]{:S(2)}, u32[]{:S(2)}) collective-permute-start(f32[16,8,512]{2,1,0:T(8,128)S(1)} %all-to-all-done), channel_id=1, source_target_pairs={{0,1},{1,0},{2,3},{3,2},{4,5},{5,4},{6,7},{7,6},{8,9},{9,8},{10,11... | collective-permute-start | bytes 786440 | tf_op jit(solution)/shard_map/ppermute | solution.py:160
  25.3 0.7 compare_select_fusion.3
  26.0 0.8 collective-permute-done
  26.8 2.8 %pick.1 = f32[8,256]{1,0:T(8,128)S(1)} custom-call(f32[32,8,512]{2,1,0:T(8,128)S(1)} %constant_dynamic-update-slice_fusion.slab_ref, s32[2,256]{1,0:T(2,128)S(1)} %pad_add_fusion.place_ref), custom_call_target="tpu_custom_call" | custom-call | tf_op jit(solution)/shard_map/pick/pallas_call | solution.py:170
  29.6 0.7 broadcast_in_dim.12
  30.2 8.8 %all-to-all-start.1 = ((f32[16,8,256]{2,1,0:T(8,128)}), f32[16,8,256]{2,1,0:T(8,128)S(1)}, u32[]{:S(2)}, u32[]{:S(2)}) async-start(f32[16,8,256]{2,1,0:T(8,128)} %broadcast_in_dim.12), calls=%async_computation.1 | async-start | bytes 262144 | tf_op jit(solution)/shard_map/all_to_all | solution.py:150
  39.0 0.9 %field.1 = (bf16[32,16384]{1,0:T(8,128)(2,1)S(1)}, bf16[48,16384]{1,0:T(8,128)(2,1)S(1)}, f32[8,128]{1,0:T(8,128)S(1)}) custom-call(f32[32,8,512]{2,1,0:T(8,128)S(1)} %constant_dynamic-update-slice_fusion.slab_ref), custom_call_target="tpu_custom_call" | custom-call | tf_op jit(solution)/shard_map/field/pallas_call | solution.py:172
  39.9 10.4 %all-to-all-done.1.picks_ref = f32[16,8,256]{2,1,0:T(8,128)S(1)} async-done(((f32[16,8,256]{2,1,0:T(8,128)}), f32[16,8,256]{2,1,0:T(8,128)S(1)}, u32[]{:S(2)}, u32[]{:S(2)}) %all-to-all-start.1) | async-done | bytes 131104 | tf_op jit(solution)/shard_map/all_to_all | solution.py:150
  50.3 20.4 %pairs.1 = f32[8,256]{1,0:T(8,128)S(1)} custom-call(f32[32,8,512]{2,1,0:T(8,128)S(1)} %constant_dynamic-update-slice_fusion.slab_ref, bf16[32,16384]{1,0:T(8,128)(2,1)S(1)} %get-tuple-element.5.sums_ref, bf16[48,16384]{1,0:T(8,128)(2,1)S(1)} %get-tuple-element.6.dots_ref, f32[8,128]{1,0:T(8,128)S(1)} %get-tuple-element.7.centre_ref, ...), custom_call_target="tpu_custom_call" | custom-call | tf_op jit(solution)/shard_map/pairs/pallas_call | solution.py:182
  70.7 13.4 %all_to_all.15 = f32[16,6,256]{2,1,0:T(8,128)S(1)} all-to-all(f32[16,6,256]{2,1,0:T(8,128)S(1)} %broadcast_in_dim.13), channel_id=1, replica_groups=mesh['x'=4,'yh'=4,'yl'=2,'z'=8,'c'=2] {'x','yh'}, dimensions={0} | all-to-all | bytes 196608 | tf_op jit(solution)/shard_map/all_to_all | solution.py:150
  84.2 0.6 fusion.2
  (6 shorter events, 0.1 us)
Async XLA Ops:
  2.2 21.1 %all-to-all-start = ((f32[16,8,512]{2,1,0:T(8,128)}), f32[16,8,512]{2,1,0:T(8,128)S(1)}, u32[]{:S(2)}, u32[]{:S(2)}) async-start(f32[16,8,512]{2,1,0:T(8,128)} %broadcast_in_dim.11), calls=%async_computation | async-start | bytes 524288 | tf_op jit(solution)/shard_map/all_to_all | solution.py:150
  23.4 3.4 %collective-permute-start = (f32[16,8,512]{2,1,0:T(8,128)S(1)}, f32[16,8,512]{2,1,0:T(8,128)S(1)}, u32[]{:S(2)}, u32[]{:S(2)}) collective-permute-start(f32[16,8,512]{2,1,0:T(8,128)S(1)} %all-to-all-done), channel_id=1, source_target_pairs={{0,1},{1,0},{2,3},{3,2},{4,5},{5,4},{6,7},{7,6},{8,9},{9,8},{10,11... | collective-permute-start | bytes 786440 | tf_op jit(solution)/shard_map/ppermute | solution.py:160
  30.2 20.1 %all-to-all-start.1 = ((f32[16,8,256]{2,1,0:T(8,128)}), f32[16,8,256]{2,1,0:T(8,128)S(1)}, u32[]{:S(2)}, u32[]{:S(2)}) async-start(f32[16,8,256]{2,1,0:T(8,128)} %broadcast_in_dim.12), calls=%async_computation.1 | async-start | bytes 262144 | tf_op jit(solution)/shard_map/all_to_all | solution.py:150

commit v2 on v0

v2 whole, which is shorter than its diff:
```python
import jax
import jax.numpy as jnp
from jax import lax
from jax.experimental import pallas as pl
from jax.experimental.pallas import tpu as pltpu
from jax.sharding import Mesh, PartitionSpec as P

SOFTEN_SQ = 0.0001
NAMES = ("x", "yh", "yl", "z", "c")
ROW = ("x", "yh")
COL = ("yl", "z", "c")
LANES = 128
TILE = 256
STEP = 16
SPAN = 32
SPANS = LANES // SPAN
GROUPS = 2
SLOTS = 2
COARSE = 1.5 * 2.0**19
MIDDLE = 1.5 * 2.0**11
F32 = jnp.float32
BF16 = jnp.bfloat16
HBM = pl.BlockSpec(memory_space=pltpu.HBM)
VMEM = pl.BlockSpec(memory_space=pltpu.VMEM)


def pieces(value):
    high = value.astype(BF16)
    rest = value - high.astype(F32)
    middle = rest.astype(BF16)
    low = (rest - middle.astype(F32)).astype(BF16)
    return high, middle, low


def copies_kernel(phase_ref, masses_ref, out_ref, block, sems):
    loads = [
        pltpu.make_async_copy(phase_ref, block.at[0:6, :], sems.at[0]),
        pltpu.make_async_copy(masses_ref, block.at[6:7, :], sems.at[1]),
    ]
    for load in loads:
        load.start()
    block[7:8, :] = jnp.zeros((1, block.shape[1]), F32)
    for load in loads:
        load.wait()
    for n in range(out_ref.shape[0]):
        out_ref[n] = block[...]


def pick_kernel(
    half_ref, other_ref, index_hbm, picks_ref, own_ref, hits_ref, index_ref, sem
):
    blocks, _, width = half_ref.shape
    count = index_ref.shape[1]
    load = pltpu.make_async_copy(index_hbm, index_ref, sem.at[0])
    load.start()
    values = []
    for c in range(7):
        both = jnp.concatenate([half_ref[:, c, :], other_ref[:, c, :]], axis=0)
        values.append(jnp.concatenate(pieces(both), axis=0))
    load.wait()
    index = index_ref[...]
    column = index // width
    place = index - column * width
    row = column // (2 * blocks)
    column = column - row * (2 * blocks)
    block = column // 2
    block = jnp.where(column - 2 * block == lax.axis_index("c"), block, block + blocks)
    here_row = lax.axis_index("x") * lax.axis_size("yh") + lax.axis_index("yh")
    block = jnp.where(row == here_row, block, -1)
    one_hot = lax.broadcasted_iota(jnp.int32, (2 * blocks, count), 0) == block
    one_hot = jnp.where(one_hot, 1.0, 0.0).astype(BF16)
    three = jnp.concatenate([one_hot, one_hot, one_hot], axis=0)
    here = lax.broadcasted_iota(jnp.int32, (width, count), 0) == place
    rows = []
    for c in range(7):
        taken = lax.dot_general(
            values[c], three, (((0,), (0,)), ((), ())), preferred_element_type=F32
        )
        rows.append(jnp.sum(jnp.where(here, taken, 0.0), axis=0, keepdims=True))
    zero = jnp.zeros((1, count), F32)
    own_ref[...] = jnp.concatenate(rows + [zero], axis=0)
    state = jnp.concatenate(rows[0:6], axis=0)
    for n in range(picks_ref.shape[0]):
        picks_ref[n] = state
    here = jnp.where(here, 1.0, 0.0).astype(BF16)
    hits_ref[...] = lax.dot_general(
        one_hot, here, (((1,), (1,)), ((), ())), preferred_element_type=F32
    )


def levels(position):
    coarse = (position + COARSE) - COARSE
    rest = position - coarse
    middle = (rest + MIDDLE) - MIDDLE
    return coarse, middle, (rest - middle).astype(BF16).astype(F32)


def squares(coarse, middle, fine):
    rest = middle + fine
    first = jnp.sum(coarse * coarse, axis=0, keepdims=True)
    second = 2.0 * jnp.sum(coarse * middle, axis=0, keepdims=True)
    third = jnp.sum(rest * rest + 2.0 * coarse * fine, axis=0, keepdims=True)
    return first, second, third


def wide(parts):
    return [part.astype(F32) for part in parts]


def field_kernel(half_ref, other_ref, own_ref, hits_ref, dots_ref, near_ref, sums_ref, centre_ref):
    blocks, _, width = half_ref.shape
    total = jnp.zeros((8, width), F32)
    for b in range(blocks):
        total = total + (half_ref[b] + other_ref[b])
    mean = jnp.sum(total, axis=1, keepdims=True) * (1.0 / (2 * blocks * width))
    centre = jnp.where(lax.broadcasted_iota(jnp.int32, (8, 1), 0) < 6, mean, 0.0)
    centre_ref[...] = jnp.broadcast_to(centre, (8, LANES))

    def block_terms(raw, mass, at):
        size = raw.shape[1]
        rows = lax.broadcasted_iota(jnp.int32, (8, size), 0)
        star = raw - centre
        where = pl.ds(pl.multiple_of(at, size), size)
        sums_ref[:, where] = jnp.where(rows == 6, mass, star * mass)
        along = jnp.sum(star[0:3, :] * star[3:6, :], axis=0, keepdims=True)
        terms = jnp.where(rows == 6, along, star)
        terms = jnp.where(rows == 7, 1.0, terms)
        high, middle, low = wide(pieces(terms))
        dot = jnp.concatenate([high, middle, low, high], axis=0)
        coarse, middle, fine = levels(raw[0:3, :])
        first, second, third = squares(coarse, middle, fine)
        first, second = wide(pieces(first)), wide(pieces(second))
        third = wide(pieces(third + SOFTEN_SQ))
        one, zero = jnp.ones_like(mass), jnp.zeros((3, size), F32)
        near = [coarse, one, first[0], first[1], second[0], second[1]]
        near += [middle, one, middle, one, fine, one]
        near += [coarse, third[0], fine, third[1], third[2], zero]
        near = jnp.concatenate(near, axis=0)
        cuts = [slice(n, n + TILE) for n in range(0, size, TILE)]
        return [dot[:, cut] for cut in cuts], [near[:, cut] for cut in cuts]

    def left(spans):
        spans = spans + [jnp.zeros_like(spans[0])] * (SPANS - len(spans))
        return jnp.transpose(jnp.concatenate(spans, axis=0)).astype(BF16)

    per = SPANS * TILE // width

    def step(i, _):
        for side, ref in enumerate((half_ref, other_ref)):
            at = i + side * (blocks // per)
            dots, nears = [], []
            for k in range(per):
                raw = ref[i * per + k]
                n = at * per + k
                mass = raw[6:7, :] * (1.0 - hits_ref[pl.ds(n, 1), :])
                dot, near = block_terms(raw, mass, n * width)
                dots += dot
                nears += near
            dots_ref[at] = left(dots)
            near_ref[at] = left(nears)
        return 0

    lax.fori_loop(0, blocks // per, step, 0)
    own = own_ref[...]
    dots, nears = block_terms(own, own[6:7, :], 2 * blocks * width)
    dots_ref[dots_ref.shape[0] - 1] = left(dots)
    near_ref[near_ref.shape[0] - 1] = left(nears)


def pair_kernel(dots_ref, near_ref, sums_ref, centre_ref, picks_ref, out_ref, dot_right, near_right, parts):
    count = picks_ref.shape[2]
    groups = dots_ref.shape[0] - 1
    state = picks_ref[0]
    for n in range(1, picks_ref.shape[0]):
        state = state + picks_ref[n]
    local = state - centre_ref[0:6, 0:1]
    position, velocity = local[0:3, :], local[3:6, :]
    along = jnp.sum(position * velocity, axis=0, keepdims=True)
    one, zero = jnp.ones((1, count), F32), jnp.zeros((1, count), F32)
    high, middle, low = wide(
        pieces(jnp.concatenate([-velocity, -position, one, along], axis=0))
    )
    none = jnp.zeros_like(high)
    dot_rows = (
        jnp.concatenate([high, high, high, middle], axis=0),
        jnp.concatenate([low, middle, none, none], axis=0),
    )
    split = levels(state[0:3, :])
    first, second, third = (wide(pieces(part)) for part in squares(*split))
    coarse, middle, fine = (-2.0 * part for part in split)
    none = jnp.zeros((3, count), F32)
    near_rows = (
        jnp.concatenate(
            [coarse, first[0], one, one, one, one, coarse, second[0], middle, third[0]]
            + [middle, third[2], fine, one, coarse, one, one, none],
            axis=0,
        ),
        jnp.concatenate(
            [middle, first[1], zero, none, none, second[1], fine, third[1], fine, zero]
            + [zero, none] * 3,
            axis=0,
        ),
    )
    for right, (rows, more) in ((dot_right, dot_rows), (near_right, near_rows)):
        none = jnp.zeros_like(rows)
        for n in range(SPANS):
            both = [rows if m == n else none for m in range(SPANS)]
            both += [more if m == n else none for m in range(SPANS)]
            right[n] = jnp.concatenate(both, axis=0).astype(BF16)

    steps = TILE // STEP

    def sums_of(total_w, total_r, dots, nears):
        planes = ((near_ref, near_right, 1, nears), (dots_ref, dot_right, 0, dots))

        def stage(tile):
            for _, right, m, _ in planes:
                pltpu.matmul_push_rhs(right[tile % SPANS], 0, m)

        def product(group, tile, t):
            block = group + tile // SPANS
            for left_ref, _, _, results in planes:
                rows = left_ref[block, t * STEP:(t + 1) * STEP, :]
                pltpu.matmul_acc_lhs(
                    results[tile % SLOTS][t],
                    jnp.concatenate([rows, rows], axis=1),
                    load_staged_rhs=0 if t == 0 else None,
                )

        def pairs(tile, t, masked):
            inverse = lax.rsqrt(pltpu.matmul_pop(nears[tile % SLOTS][t]))
            inverse_sq = inverse * inverse
            weight = inverse * inverse_sq
            if masked:
                star = lax.broadcasted_iota(jnp.int32, (STEP, TILE), 0) + t * STEP
                active_star = lax.broadcasted_iota(jnp.int32, (STEP, TILE), 1)
                weight = jnp.where(star == active_star, 0.0, weight)
            rate = weight * (pltpu.matmul_pop(dots[tile % SLOTS][t]) * inverse_sq)
            rows = slice(t * STEP, (t + 1) * STEP)
            for m, value in enumerate((weight, rate)):
                high = value.astype(BF16)
                parts[tile % 2, m, 0, rows, :] = high
                parts[tile % 2, m, 1, rows, :] = (value - high.astype(F32)).astype(BF16)

        def stage_parts(tile):
            for n in range(2):
                for m in range(2):
                    pltpu.matmul_push_rhs(parts[tile % 2, m, n], 1 - n, m)

        def add(number):
            start = pl.multiple_of(jnp.maximum(number, 0) * TILE, TILE)
            field = pieces(sums_ref[:, pl.ds(start, TILE)])
            field = jnp.concatenate(field + (jnp.zeros_like(field[0]),), axis=0)
            for n in range(2):
                for m, total in enumerate((total_w, total_r)):
                    pltpu.matmul_acc_lhs(total, field, load_staged_rhs=1 - n)

        parts[1] = jnp.zeros_like(parts[1])
        stage(0)
        for t in range(steps):
            product(0, 0, t)
        stage(1)
        tiles = GROUPS * SPANS

        def step(i, _):
            for tile in range(tiles):
                product(i * GROUPS, tile + 1, 0)
                stage_parts(tile + 1)
                pairs(tile, 0, False)
                for t in range(1, steps):
                    product(i * GROUPS, tile + 1, t)
                    pairs(tile, t, False)
                add(i * tiles + tile - 1)
                stage(tile + 2)
            return 0

        lax.fori_loop(0, groups // GROUPS, step, 0)
        product(groups, 1, 0)
        for results in (nears, dots):
            pltpu.matmul_pop(results[1 % SLOTS][0])
        stage_parts(1)
        for t in range(steps):
            pairs(0, t, True)
        add(groups * SPANS - 1)
        stage_parts(0)
        add(groups * SPANS)
        sums = pltpu.matmul_pop(total_w)
        rates = pltpu.matmul_pop(total_r)
        sums = sums[0:8, :] + sums[8:16, :] + sums[16:24, :]
        rates = rates[0:8, :] + rates[8:16, :] + rates[16:24, :]
        accel = sums[0:3, :] - position * sums[6:7, :]
        jerk = sums[3:6, :] - velocity * sums[6:7, :]
        jerk = jerk - 3.0 * (rates[0:3, :] - position * rates[6:7, :])
        both = jnp.concatenate([accel, jerk], axis=0)
        for n in range(out_ref.shape[0]):
            out_ref[n] = both

    def results(m):
        return [[pltpu.ACC(m)((STEP, TILE), F32) for _ in range(steps)] for _ in range(SLOTS)]

    pl.run_scoped(
        sums_of,
        pltpu.ACC(0)((32, TILE), F32),
        pltpu.ACC(1)((32, TILE), F32),
        results(0),
        results(1),
    )


def call(kernel, name, outs, scratch=(), ins=None):
    more = {} if ins is None else {"in_specs": ins}
    return pl.pallas_call(
        kernel,
        out_shape=outs,
        **more,
        scratch_shapes=list(scratch),
        compiler_params=pltpu.CompilerParams(vmem_limit_bytes=40 * 2**20),
        name=name,
    )


def shape(*sizes, dtype=F32):
    return jax.ShapeDtypeStruct(sizes, dtype)


def local(phase, masses, active_index):
    width = phase.shape[1]
    count = active_index.shape[0]
    rows_count, cols_count = lax.axis_size(ROW), lax.axis_size(COL)
    stars = width * rows_count * cols_count
    near = ("yl", "z")
    near_count = lax.axis_size(near)

    copies = call(
        copies_kernel,
        "copies",
        shape(near_count, 8, width),
        (pltpu.VMEM((8, width), F32), pltpu.SemaphoreType.DMA((2,))),
        [HBM, HBM],
    )(phase, masses)
    half = lax.all_to_all(copies, near, 0, 0)
    other = lax.ppermute(half, "c", [(0, 1), (1, 0)])
    picks, own, hits = call(
        pick_kernel,
        "pick",
        (shape(rows_count, 6, count), shape(8, count), shape(cols_count, width)),
        (pltpu.VMEM((1, count), jnp.int32), pltpu.SemaphoreType.DMA((1,))),
        [VMEM, VMEM, HBM],
    )(half, other, active_index.reshape(1, count))
    picks = lax.all_to_all(picks, ROW, 0, 0)
    factor = shape(cols_count * width // (TILE * SPANS) + 1, TILE, LANES, dtype=BF16)
    dots, near, sums, centre = call(
        field_kernel,
        "field",
        (factor, factor, shape(8, cols_count * width + count), shape(8, LANES)),
    )(half, other, own, hits)
    right = pltpu.VMEM((SPANS, TILE, count), BF16)
    parts = pltpu.VMEM((2, 2, 2, TILE, count), BF16)
    partial = call(pair_kernel, "pairs", shape(rows_count, 6, count), (right, right, parts))(
        dots, near, sums, centre, picks
    )
    total = jnp.sum(lax.all_to_all(partial, ROW, 0, 0), axis=0) * (1.0 / stars)
    return total[0:3], total[3:6]


def solution(mesh):
    fine = Mesh(mesh.devices.reshape(4, 4, 2, 8, 2), NAMES)
    stars = P(None, ROW + COL)
    return jax.shard_map(
        local,
        mesh=fine,
        in_specs=(stars, stars, P(COL)),
        out_specs=(P(None, COL), P(None, COL)),
        check_vma=False,
    )
```

time: 465 us -> 73.6 us (0.16)
  waiting for transfers between devices: 249 us -> 10.3 us
  blocking collectives: 117 us -> 34.4 us
  other arithmetic: 50.6 us -> 0.03 us
  local copies, waits for them, and re-layouts: 31.9 us -> 2.67 us
  Pallas kernels: 0 us -> 14.4 us
  between operations: 14.1 us -> 0.68 us
  starting transfers between devices: 0.04 us -> 10.7 us
    psum x1 -> x0, waiting for transfers between devices: 249 us -> none  [local(): active_table = lax.psum(picked, ('row', 'col'))]
    all_gather x2 -> x0, blocking collectives: 71.8 us -> none  [the longest x1 39.6 us: local(): all_index = lax.all_gather(active_index, 'col', axis=0, tiled=True)]
    psum x1 -> x0, blocking collectives: 45.4 us -> none  [local(): total = lax.psum(partial_sum, 'row')]
    reduce_sum x64 -> x1, other arithmetic: 35.7 us -> 0.02 us  [local(): total = jnp.sum(lax.all_to_all(partial, ROW, 0, 0), axis=0) * (1.0 / stars)]
    all_to_all x0 -> x2, blocking collectives: none -> 34.4 us  [the longest x1 20.9 us: local(): half = lax.all_to_all(copies, near, 0, 0)]
    gather x1 -> x0, local copies, waits for them, and re-layouts: 27.7 us -> none  [local(): jnp.take(phase, jnp.clip(local_index, 0, shard_width - 1), axis=1)]
    pallas_call x0 -> x4, Pallas kernels: none -> 14.4 us  [the longest x1 10.4 us: local(): call(pair_kernel, 'pairs', shape(rows_count, 6, count), (right, right, pa...]
    mul x2 -> x1, other arithmetic: 9.69 us -> 0.01 us  [local(): total = jnp.sum(lax.all_to_all(partial, ROW, 0, 0), axis=0) * (1.0 / stars)]
  transfers between devices with their start and end apart: 1 -> 2, of which waited for: 1 -> 2; matrix products, arithmetic and copies ran while one was open for 0% -> 0% of each run, Pallas kernels for 0% -> 3%
where the time goes in v2:
time: 73.6 us; the launch traced here: 73.2 us
  blocking collectives  34.4 us (47%)
  Pallas kernels  14.4 us (20%)
  starting transfers between devices  10.7 us (15%)
  waiting for transfers between devices  10.3 us (14%)
  local copies, waits for them, and re-layouts  2.67 us (4%)
    all_to_all x1, blocking collectives, local(): half = lax.all_to_all(copies, near, 0, 0)  20.9 us
    all_to_all x1, blocking collectives, local(): total = jnp.sum(lax.all_to_all(partial, ROW, 0, 0), axis=0) * (1.0 / stars)  13.5 us
    pallas_call x1, Pallas kernels, local(): call(pair_kernel, 'pairs', shape(rows_count, 6, count), (right, right, pa...  10.4 us
    all_to_all x1, waiting for transfers between devices, local(): picks = lax.all_to_all(picks, ROW, 0, 0)  8.8 us
    all_to_all x1, starting transfers between devices, local(): picks = lax.all_to_all(picks, ROW, 0, 0)  8.78 us
    pallas_call x1, Pallas kernels, local(): call(field_kernel, 'field', (factor, factor, shape(8, cols_count * width...  2.48 us
    unnamed x6, local copies, waits for them, and re-layouts  2.07 us
    ppermute x1, starting transfers between devices, local(): other = lax.ppermute(half, 'c', [(0, 1), (1, 0)])  1.91 us
  transfers between devices with their start and end apart: 2, of which 2 were waited for; matrix products, arithmetic and copies ran while one was open for 0% of the time, Pallas kernels for 3%

profile of v2, /device:TPU:8, one launch (start us, length us, event | category | flops | bytes accessed | tf_op | source)
XLA Modules:
  0.0 73.2 jit_solution(8135495373268082156)
XLA Ops:
  0.6 0.0 copy-start
  0.6 0.7 copy-done
  1.3 0.0 copy-start.1
  1.4 0.7 copy-done.1
  2.1 20.9 %all_to_all.15.half_ref = f32[16,8,512]{2,1,0:T(8,128)S(1)} all-to-all(f32[16,8,512]{2,1,0:T(8,128)S(1)} %copies.1), channel_id=1, replica_groups=mesh['x'=4,'yh'=4,'yl'=2,'z'=8,'c'=2] {'yl','z'}, dimensions={0} | all-to-all | bytes 524288 | tf_op jit(solution)/shard_map/all_to_all | solution.py:341
  23.0 1.9 %collective-permute-start = (f32[16,8,512]{2,1,0:T(8,128)S(1)}, f32[16,8,512]{2,1,0:T(8,128)S(1)}, u32[]{:S(2)}, u32[]{:S(2)}) collective-permute-start(f32[16,8,512]{2,1,0:T(8,128)S(1)} %all_to_all.15.half_ref), channel_id=1, source_target_pairs={{0,1},{1,0},{2,3},{3,2},{4,5},{5,4},{6,7},{7,6},{8,9},{9,8},{10,11... | collective-permute-start | bytes 786440 | tf_op jit(solution)/shard_map/ppermute | solution.py:342
  24.9 1.5 %collective-permute-done.other_ref = f32[16,8,512]{2,1,0:T(8,128)S(1)} collective-permute-done((f32[16,8,512]{2,1,0:T(8,128)S(1)}, f32[16,8,512]{2,1,0:T(8,128)S(1)}, u32[]{:S(2)}, u32[]{:S(2)}) %collective-permute-start) | collective-permute-done | bytes 262176 | tf_op jit(solution)/shard_map/ppermute | solution.py:342
  26.4 0.0 copy-start.2
  26.4 0.7 copy-done.2
  27.1 1.5 %pick.1 = (f32[16,6,256]{2,1,0:T(8,128)}, f32[8,256]{1,0:T(8,128)S(1)}, f32[32,512]{1,0:T(8,128)S(1)}) custom-call(f32[16,8,512]{2,1,0:T(8,128)S(1)} %all_to_all.15.half_ref, f32[16,8,512]{2,1,0:T(8,128)S(1)} %collective-permute-done.other_ref, s32[1,256]{1,0:T(1,128)S(1)} %bitcast.1), custom_call_target="tpu_custom_call" | custom-call | tf_op jit(solution)/shard_map/pick/pallas_call | solution.py:343
  28.6 8.8 %all-to-all-start.1 = ((f32[16,6,256]{2,1,0:T(8,128)}), f32[16,6,256]{2,1,0:T(8,128)S(1)}, u32[]{:S(2)}, u32[]{:S(2)}) async-start(f32[16,6,256]{2,1,0:T(8,128)} %get-tuple-element.15), calls=%async_computation.1 | async-start | bytes 262144 | tf_op jit(solution)/shard_map/all_to_all | solution.py:350
  37.4 2.5 %field.1 = (bf16[17,256,128]{2,1,0:T(8,128)(2,1)S(1)}, bf16[17,256,128]{2,1,0:T(8,128)(2,1)S(1)}, f32[8,16640]{1,0:T(8,128)S(1)}, f32[8,128]{1,0:T(8,128)S(1)}) custom-call(f32[16,8,512]{2,1,0:T(8,128)S(1)} %all_to_all.15.half_ref, f32[16,8,512]{2,1,0:T(8,128)S(1)} %collective-permute-done.other_ref, f32[8,256]{1,0:T(8,128)S(1)} %get-tuple-element.9.own_ref, ...), custom_call_target="tpu_custom_call" | custom-call | tf_op jit(solution)/shard_map/field/pallas_call | solution.py:352
  39.9 8.8 %all-to-all-done.1.picks_ref = f32[16,6,256]{2,1,0:T(8,128)S(1)} async-done(((f32[16,6,256]{2,1,0:T(8,128)}), f32[16,6,256]{2,1,0:T(8,128)S(1)}, u32[]{:S(2)}, u32[]{:S(2)}) %all-to-all-start.1) | async-done | bytes 98336 | tf_op jit(solution)/shard_map/all_to_all | solution.py:350
  48.7 10.4 %pairs.1 = f32[16,6,256]{2,1,0:T(8,128)S(1)} custom-call(bf16[17,256,128]{2,1,0:T(8,128)(2,1)S(1)} %get-tuple-element.11.dots_ref, bf16[17,256,128]{2,1,0:T(8,128)(2,1)S(1)} %get-tuple-element.12.near_ref, f32[8,16640]{1,0:T(8,128)S(1)} %get-tuple-element.13.sums_ref, f32[8,128]{1,0:T(8,128)S(1)} %get-tuple-element.14.centre_ref, ...), custom_call_target="tpu_custom_call" | custom-call | tf_op jit(solution)/shard_map/pairs/pallas_call | solution.py:359
  59.1 13.5 %all_to_all.16 = f32[16,6,256]{2,1,0:T(8,128)S(1)} all-to-all(f32[16,6,256]{2,1,0:T(8,128)S(1)} %pairs.1), channel_id=1, replica_groups=mesh['x'=4,'yh'=4,'yl'=2,'z'=8,'c'=2] {'x','yh'}, dimensions={0} | all-to-all | bytes 196608 | tf_op jit(solution)/shard_map/all_to_all | solution.py:362
  72.6 0.6 fusion
  (3 shorter events, 0.1 us)
Async XLA Ops:
  0.6 0.7 copy-start
  1.3 0.7 copy-start.1
  23.0 3.4 %collective-permute-start = (f32[16,8,512]{2,1,0:T(8,128)S(1)}, f32[16,8,512]{2,1,0:T(8,128)S(1)}, u32[]{:S(2)}, u32[]{:S(2)}) collective-permute-start(f32[16,8,512]{2,1,0:T(8,128)S(1)} %all_to_all.15.half_ref), channel_id=1, source_target_pairs={{0,1},{1,0},{2,3},{3,2},{4,5},{5,4},{6,7},{7,6},{8,9},{9,8},{10,11... | collective-permute-start | bytes 786440 | tf_op jit(solution)/shard_map/ppermute | solution.py:342
  26.4 0.7 copy-start.2
  28.6 20.1 %all-to-all-start.1 = ((f32[16,6,256]{2,1,0:T(8,128)}), f32[16,6,256]{2,1,0:T(8,128)S(1)}, u32[]{:S(2)}, u32[]{:S(2)}) async-start(f32[16,6,256]{2,1,0:T(8,128)} %get-tuple-element.15), calls=%async_computation.1 | async-start | bytes 262144 | tf_op jit(solution)/shard_map/all_to_all | solution.py:350
